TPU v7x, 32 devices: a whole 2x2x4 slice. The times are simulated.
32 devices in a mesh: narrow: 2 (over x), wide: 16 (over z, y, core).
Axes of the slice: x: 2, y: 2, z: 4, core: 2. Of those that a mesh axis runs over, the one named last changes fastest.
Arguments:
- state: float32 [1280, 1280], P('wide', 'narrow'), may hold values from 0 to 10, as said below
- in_pattern: int32 [5, 5], replicated, may hold values from 0 to 1, as said below
- out_pattern: int32 [5, 5], replicated, may hold values from 0 to 1, as said below
Outputs:
- clustered: float32 [1280, 1280], P('wide', 'narrow')
Inputs may be any that keep to these rules, and one draw needn't show every extreme that they name: `in_pattern`: entries are 0 or 1 and every diagonal block is 1. `out_pattern`: entries are 0 or 1 and every diagonal block is 1. `state`: nonnegative; the diagonal lies between 0.5 and 1.
All inputs are finite; a program needn't handle non-finite values.
Results may differ from a plain program's by a relative error of at most 0.00011.
Values sent between devices are 32-bit elements; how exact they have to be, the bound alone decides.
A program may use at most 64 MiB of HBM per device.

v0:
```python
import jax
import jax.numpy as jnp
from jax import lax
from jax.sharding import PartitionSpec as P

BLK = 256


def tile_mask(pattern, row_start, rows, col_start, cols):
    blocks = pattern.shape[0]
    row_blk = (row_start + jnp.arange(rows)) // BLK
    col_blk = (col_start + jnp.arange(cols)) // BLK
    row_pick = (row_blk[:, None] == jnp.arange(blocks)[None, :]).astype(jnp.float32)
    col_pick = (col_blk[:, None] == jnp.arange(blocks)[None, :]).astype(jnp.float32)
    picked = jnp.dot(row_pick, pattern.astype(jnp.float32), preferred_element_type=jnp.float32)
    return jnp.dot(picked, col_pick.T, preferred_element_type=jnp.float32)


def body(state, in_pattern, out_pattern):
    rows, cols = state.shape
    nodes_all = cols * lax.axis_size("narrow")
    row_start = lax.axis_index("wide") * rows
    col_start = lax.axis_index("narrow") * cols
    masked = state * tile_mask(in_pattern, row_start, rows, col_start, cols)
    column_block = lax.all_gather(masked, "wide", axis=0, tiled=True)
    expanded = jnp.dot(
        lax.all_gather(masked, "narrow", axis=1, tiled=True),
        column_block,
        preferred_element_type=jnp.float32,
        precision=lax.Precision.HIGHEST,
    )
    inflated = expanded * expanded * tile_mask(out_pattern, row_start, rows, col_start, cols)
    totals = lax.psum(jnp.sum(inflated, axis=1), "narrow")
    return inflated * (nodes_all / totals)[:, None]


def solution(mesh):
    return jax.shard_map(
        body,
        mesh=mesh,
        in_specs=(P("wide", "narrow"), P(), P()),
        out_specs=P("wide", "narrow"),
        check_vma=False,
    )
```

profile of v0, /device:TPU:0, one launch (start us, length us, event | category | flops | bytes accessed | tf_op | source)
XLA Modules:
  0.0 75.0 jit_solution(4445144862103303681)
XLA Ops:
  6.5 0.0 all-gather.2.cloned.1.call-start
  6.6 2.0 %convolution_multiply_fusion.1 = f32[80,640]{1,0:T(8,128)} fusion(f32[80,640]{1,0:T(8,128)} %param.3, s32[640]{0:T(1024)S(1)} %add_select_fusion, s32[80]{0:T(128)S(1)} %and_select_fusion, s32[5,5]{1,0:T(8,128)} %param.4), kind=kOutput, calls=%fused_computation.2 | convolution fusion | flops 570825 | bytes 412580 | tf_op jit(solution)/shard_map/dot_general | solution.py:16
  8.5 0.0 all-gather.2.cloned.1.call-update
  8.6 8.9 %all_gather.6 = f32[80,1280]{1,0:T(8,128)S(1)} all-gather(f32[80,640]{1,0:T(8,128)} %convolution_multiply_fusion.1), channel_id=1, replica_groups=mesh['narrow'=2,'wide'=16] {'narrow'}, dimensions={1}, use_global_device_ids=true | all-gather | bytes 614400 | tf_op jit(solution)/shard_map/all_gather | solution.py:27
  17.5 1.0 %fusion.3 = f32[80,640]{1,0:T(8,128)S(1)} fusion(s32[640]{0:T(1024)S(1)} %add_select_fusion, s32[80]{0:T(128)S(1)} %and_select_fusion, s32[5,5]{1,0:T(8,128)} %param.5), kind=kOutput, calls=%fused_computation.4 | convolution fusion | flops 519625 | bytes 207780 | tf_op jit(solution)/shard_map/dot_general | solution.py:16
  18.5 39.8 %all-gather.2.cloned.1.call-done = f32[1280,640]{1,0:T(8,128)} async-done(((f32[80,640]{1,0:T(8,128)}), f32[1280,640]{1,0:T(8,128)}) %all-gather.2.cloned.1.call-update) | async-done | bytes 3276816 | tf_op jit(solution)/shard_map/all_gather | solution.py:25
  58.4 4.0 %fusion.19 = (f32[80]{0:T(128)S(1)}, f32[80,640]{1,0:T(8,128)S(1)}) fusion(f32[80,640]{1,0:T(8,128)S(1)} %fusion.3, f32[80,1280]{1,0:T(8,128)S(1)} %all_gather.6, f32[1280,640]{1,0:T(8,128)} %all-gather.2.cloned.1.call-done), kind=kOutput, calls=%fused_computation.29 | convolution fusion | flops 786585536 | bytes 4096320 | tf_op jit(solution)/shard_map/dot_general | solution.py:26
  62.4 4.9 %psum.7 = f32[80]{0:T(128)S(1)} all-reduce(f32[80]{0:T(128)S(1)} %get-tuple-element.5), channel_id=1, replica_groups=mesh['narrow'=2,'wide'=16] {'narrow'}, use_global_device_ids=true, to_apply=%region_1.2 | all-reduce | flops 80 | bytes 640 | tf_op jit(solution)/shard_map/psum | solution.py:33
  67.4 0.8 %broadcast_multiply_fusion = f32[80,640]{1,0:T(8,128)} fusion(f32[80,640]{1,0:T(8,128)S(1)} %get-tuple-element.6, f32[80]{0:T(128)S(1)} %broadcast_divide_fusion), kind=kLoop, calls=%fused_computation.9 | loop fusion | flops 51200 | bytes 409920 | tf_op jit(solution)/shard_map/mul | solution.py:34
  (3 shorter events, 0.0 us)
Async XLA Ops:
  6.5 51.9 %all-gather.2.cloned.1.call-start = ((), (), s32[]{:S(2)}) async-start(), calls=%async_computation | async-start | bytes 3481600 | tf_op jit(solution)/shard_map/all_gather | solution.py:25
Sparse Core Ops, SparseCore 0:
  9.6 48.7 all-gather.1
where the time goes:
time: 75.2 us; the launch traced here: 75 us
  waiting for transfers between devices  39.9 us (53%)
  blocking collectives  13.9 us (18%)
  between operations  13.4 us (18%)
  matrix products  7.02 us (9%)
  other arithmetic  0.8 us (1%)
    all_gather x1, waiting for transfers between devices, body(): column_block = lax.all_gather(masked, 'wide', axis=0, tiled=True)  39.8 us
    all_gather x1, blocking collectives, body(): lax.all_gather(masked, 'narrow', axis=1, tiled=True)  8.94 us
    psum x1, blocking collectives, body(): totals = lax.psum(jnp.sum(inflated, axis=1), 'narrow')  4.94 us
    dot_general x1, matrix products, body(): jnp.dot(lax.all_gather(masked, 'narrow', axis=1, tiled=True), column_bloc...  4.01 us
    dot_general x2, matrix products, tile_mask(): return jnp.dot(picked, col_pick.T, preferred_element_type=jnp.float32)  3.01 us
  transfers between devices with their start and end apart: 1, of which 1 were waited for; matrix products, arithmetic and copies ran while one was open for 1% of the time, Pallas kernels for 0%

commit v1 on v0

v1 whole, which is shorter than its diff:
```python
import functools

import jax
import jax.numpy as jnp
from jax import lax
from jax.experimental import pallas as pl
from jax.experimental.pallas import tpu as pltpu
from jax.sharding import PartitionSpec as P

BLK = 256
LANES = 128
MESH = pl.DeviceIdType.MESH
UP, DOWN, ACROSS, SIBLING = range(4)


def split(value):
    high = value.astype(jnp.bfloat16)
    low = (value - high.astype(jnp.float32)).astype(jnp.bfloat16)
    return high, low


def kernel(
    narrow, wide, parts, in_ref, out_pat_ref, x_ref, o_ref,
    blocks, row_parts, sums, send_sem, recv_sem,
    row_send, row_recv, sum_send, sum_recv,
):
    rows, cols = x_ref.shape
    blks = in_ref.shape[0]
    units = cols // LANES
    line = wide // 4
    group = wide // narrow
    n = lax.axis_index("narrow")
    w = lax.axis_index("wide")
    z, y, c = w // 4, (w // 2) % 2, w % 2

    def index(zz, yy, cc):
        return (zz * 2 + yy) * 2 + cc

    def partner(kind):
        return {
            UP: (n, index(z + 1, y, c)),
            DOWN: (n, index(z - 1, y, c)),
            ACROSS: (n, index(z, 1 - y, c)),
            SIBLING: (n, index(z, y, 1 - c)),
        }[kind]

    has_up, has_down = z + 1 < line, z >= 1
    others = [lax.rem(n + d, narrow) for d in range(1, narrow)]

    barrier = pltpu.get_barrier_semaphore()

    def greet(device):
        pl.semaphore_signal(barrier, inc=1, device_id=device, device_id_type=MESH)

    greet(partner(ACROSS))
    greet(partner(SIBLING))
    for other in others:
        greet((other, w))

    @pl.when(has_up)
    def _():
        greet(partner(UP))

    @pl.when(has_down)
    def _():
        greet(partner(DOWN))

    first = (w * rows) // BLK
    second = jnp.minimum(first + 1, blks - 1)
    upper = lax.broadcasted_iota(jnp.int32, (rows, LANES), 0) < (first + 1) * BLK - w * rows

    def keep(pattern, u):
        col = (n * cols + u * LANES) // BLK
        return jnp.where(
            upper, pattern[first, col].astype(jnp.float32), pattern[second, col].astype(jnp.float32)
        )

    for u in range(units):
        at = slice(u * LANES, (u + 1) * LANES)
        masked = x_ref[:, at] * keep(in_ref, u)
        blocks[w, :, at] = masked
        row_parts[n, :, at] = masked

    met = 1 + 1 + len(others) + has_up.astype(jnp.int32) + has_down.astype(jnp.int32)
    pl.semaphore_wait(barrier, met)

    def copy(kind, slot, part):
        start, size, _ = parts[part]
        ref = blocks.at[slot, pl.ds(start, size), :]
        return pltpu.make_async_remote_copy(
            src_ref=ref,
            dst_ref=ref,
            send_sem=send_sem.at[kind, slot, part],
            recv_sem=recv_sem.at[slot, part],
            device_id=partner(kind),
            device_id_type=MESH,
        )

    def arrive(slot, part):
        copy(SIBLING, slot, part).wait_recv()

    def go(kind, slot, part, act):
        if kind == UP:
            pl.when(has_up)(lambda: act(copy(kind, slot, part)))
        elif kind == DOWN:
            pl.when(has_down)(lambda: act(copy(kind, slot, part)))
        else:
            act(copy(kind, slot, part))

    def row_copy(other):
        return pltpu.make_async_remote_copy(
            src_ref=blocks.at[w],
            dst_ref=row_parts.at[n],
            send_sem=row_send.at[other],
            recv_sem=row_recv.at[n],
            device_id=(other, w),
            device_id_type=MESH,
        )

    def row_arrival(other):
        return pltpu.make_async_remote_copy(
            src_ref=blocks.at[w],
            dst_ref=row_parts.at[other],
            send_sem=row_send.at[other],
            recv_sem=row_recv.at[other],
            device_id=(other, w),
            device_id_type=MESH,
        )

    def walk(visit):
        count = len(parts)
        for part in range(count):
            visit(None, w, part, (UP, DOWN, ACROSS, SIBLING), True)
        across = [p for p in range(count) if parts[p][2]]
        along = [p for p in range(count) if not parts[p][2]]
        for part in across:
            visit(None, index(z, 1 - y, c), part, (UP, DOWN, SIBLING), False)
        for part in along:
            visit(None, index(z, 1 - y, c), part, (SIBLING,), False)
        for step in range(1, line):
            for part in along:
                visit(z >= step, index(z - step, y, c), part, (UP, ACROSS, SIBLING), False)
                visit(z + step < line, index(z + step, y, c), part, (DOWN, ACROSS, SIBLING), False)
            for part in across:
                for yy in (y, 1 - y):
                    visit(z >= step, index(z - step, yy, c), part, (UP, SIBLING), False)
                    visit(z + step < line, index(z + step, yy, c), part, (DOWN, SIBLING), False)
            for part in along:
                visit(z >= step, index(z - step, 1 - y, c), part, (SIBLING,), False)
                visit(z + step < line, index(z + step, 1 - y, c), part, (SIBLING,), False)

    def under(condition, act):
        if condition is None:
            act()
        else:
            pl.when(condition)(act)

    def forward(condition, slot, part, kinds, mine):
        def act():
            if not mine:
                arrive(slot, part)
            for kind in kinds:
                go(kind, slot, part, lambda one: one.start())

        under(condition, act)
        if mine and part == len(parts) - 1:
            for other in others:
                row_copy(other).start()

    walk(forward)
    for zz in range(line):
        for yy in range(2):
            for part in range(len(parts)):
                arrive(index(zz, yy, 1 - c), part)
    for other in others:
        row_arrival(other).wait_recv()

    expanded = None
    for g in range(narrow):
        a_high, a_low = split(row_parts[g])
        both = jnp.concatenate([a_high, a_low], axis=0)
        b_high, b_low = split(blocks[pl.ds(g * group, group)].reshape(group * rows, cols))
        first_two = jnp.dot(both, b_high, preferred_element_type=jnp.float32)
        term = first_two[:rows] + first_two[rows:]
        term = term + jnp.dot(a_high, b_low, preferred_element_type=jnp.float32)
        expanded = term if expanded is None else expanded + term

    partial = None
    for u in range(units):
        at = slice(u * LANES, (u + 1) * LANES)
        inflated = expanded[:, at] * expanded[:, at] * keep(out_pat_ref, u)
        o_ref[:, at] = inflated
        partial = inflated if partial is None else partial + inflated
    sums[n] = partial

    def sum_copy(other, slot):
        return pltpu.make_async_remote_copy(
            src_ref=sums.at[n],
            dst_ref=sums.at[slot],
            send_sem=sum_send.at[other],
            recv_sem=sum_recv.at[slot],
            device_id=(other, w),
            device_id_type=MESH,
        )

    for other in others:
        sum_copy(other, n).start()

    def drain(condition, slot, part, kinds, mine):
        under(condition, lambda: [go(kind, slot, part, lambda one: one.wait_send()) for kind in kinds] and None)

    walk(drain)
    for other in others:
        row_copy(other).wait_send()
    for other in others:
        sum_copy(other, other).wait_recv()
    total = sums[0]
    for g in range(1, narrow):
        total = total + sums[g]
    scale = (cols * narrow) / jnp.sum(total, axis=1, keepdims=True)
    o_ref[...] = o_ref[...] * scale
    for other in others:
        sum_copy(other, n).wait_send()


def body(narrow, wide, state, in_pattern, out_pattern):
    rows, cols = state.shape
    part = rows // 80 * 64 if rows % 80 == 0 else rows // 2
    parts = ((0, part, False), (part, rows - part, True))
    smem = pl.BlockSpec(memory_space=pltpu.SMEM)
    vmem = pl.BlockSpec(memory_space=pltpu.VMEM)
    flops = 2 * rows * cols * cols * narrow
    return pl.pallas_call(
        functools.partial(kernel, narrow, wide, parts),
        out_shape=jax.ShapeDtypeStruct((rows, cols), jnp.float32),
        in_specs=[smem, smem, vmem],
        out_specs=vmem,
        scratch_shapes=[
            pltpu.VMEM((wide, rows, cols), jnp.float32),
            pltpu.VMEM((narrow, rows, cols), jnp.float32),
            pltpu.VMEM((narrow, rows, LANES), jnp.float32),
            pltpu.SemaphoreType.DMA((4, wide, len(parts))),
            pltpu.SemaphoreType.DMA((wide, len(parts))),
            pltpu.SemaphoreType.DMA((narrow,)),
            pltpu.SemaphoreType.DMA((narrow,)),
            pltpu.SemaphoreType.DMA((narrow,)),
            pltpu.SemaphoreType.DMA((narrow,)),
        ],
        compiler_params=pltpu.CompilerParams(
            collective_id=0, has_side_effects=True, vmem_limit_bytes=48 * 1024 * 1024
        ),
        cost_estimate=pl.CostEstimate(flops=flops, bytes_accessed=8 * rows * cols, transcendentals=0),
    )(in_pattern, out_pattern, state)


def solution(mesh):
    return jax.shard_map(
        functools.partial(body, mesh.shape["narrow"], mesh.shape["wide"]),
        mesh=mesh,
        in_specs=(P("wide", "narrow"), P(), P()),
        out_specs=P("wide", "narrow"),
        check_vma=False,
    )
```

time: 75.2 us -> 36.5 us (0.49)
  waiting for transfers between devices: 39.9 us -> 0 us
  Pallas kernels: 0 us -> 33.3 us
  blocking collectives: 13.9 us -> 0 us
  between operations: 13.4 us -> 0.01 us
  matrix products: 7.02 us -> 0 us
  local copies, waits for them, and re-layouts: 0 us -> 2.98 us
  other arithmetic: 0.8 us -> 0 us
    all_gather x1 -> x0, waiting for transfers between devices: 39.8 us -> none  [body(): column_block = lax.all_gather(masked, 'wide', axis=0, tiled=True)]
    pallas_call x0 -> x1, Pallas kernels: none -> 33.3 us  [body(): pl.pallas_call(functools.partial(kernel, narrow, wide, parts), out_shape=...]
    all_gather x1 -> x0, blocking collectives: 8.94 us -> none  [body(): lax.all_gather(masked, 'narrow', axis=1, tiled=True)]
    dot_general x3 -> x0, matrix products: 7.02 us -> none  [the longest x1 4.01 us: body(): jnp.dot(lax.all_gather(masked, 'narrow', axis=1, tiled=True), column_bloc...]
    psum x1 -> x0, blocking collectives: 4.94 us -> none  [body(): totals = lax.psum(jnp.sum(inflated, axis=1), 'narrow')]
    unnamed x0 -> x7, local copies, waits for them, and re-layouts: none -> 2.98 us
    mul x1 -> x0, other arithmetic: 0.77 us -> none  [body(): return inflated * (nodes_all / totals)[:, None]]
  transfers between devices with their start and end apart: 1 -> 0, of which waited for: 1 -> 0; matrix products, arithmetic and copies ran while one was open for 1% -> 0% of each run, Pallas kernels for 0% -> 0%
where the time goes in v1:
time: 36.5 us; the launch traced here: 36.3 us
  Pallas kernels  33.3 us (91%)
  local copies, waits for them, and re-layouts  2.98 us (8%)
    pallas_call x1, Pallas kernels, body(): pl.pallas_call(functools.partial(kernel, narrow, wide, parts), out_shape=...  33.3 us
    unnamed x7, local copies, waits for them, and re-layouts  2.98 us

profile of v1, /device:TPU:0, one launch (start us, length us, event | category | flops | bytes accessed | tf_op | source)
XLA Modules:
  0.0 36.3 jit_solution(11292042628776254986)
XLA Ops:
  0.0 0.0 copy-start
  0.0 0.9 %copy-done = f32[80,640]{1,0:T(8,128)S(1)} copy-done((f32[80,640]{1,0:T(8,128)S(1)}, f32[80,640]{1,0:T(8,128)}, u32[]{:S(2)}) %copy-start) | copy-done | bytes 204824
  0.9 0.0 copy-start.1
  0.9 0.7 %copy-done.1 = s32[5,5]{1,0:T(8,128)S(1)} copy-done((s32[5,5]{1,0:T(8,128)S(1)}, s32[5,5]{1,0:T(8,128)}, u32[]{:S(2)}) %copy-start.1) | copy-done | bytes 124
  1.6 0.0 copy-start.2
  1.6 0.7 %copy-done.2 = s32[5,5]{1,0:T(8,128)S(1)} copy-done((s32[5,5]{1,0:T(8,128)S(1)}, s32[5,5]{1,0:T(8,128)}, u32[]{:S(2)}) %copy-start.2) | copy-done | bytes 124
  2.3 33.3 %shard_map.37 = f32[80,640]{1,0:T(8,128)S(1)} custom-call(s32[5,5]{1,0:T(8,128)S(1)} %copy-done.1, s32[5,5]{1,0:T(8,128)S(1)} %copy-done.2, f32[80,640]{1,0:T(8,128)S(1)} %copy-done), custom_call_target="tpu_custom_call" | custom-call | flops 131072000 | bytes 409600 | tf_op jit(solution)/shard_map/pallas_call | solution.py:233
  35.6 0.7 %copy.5 = f32[80,640]{1,0:T(8,128)} copy(f32[80,640]{1,0:T(8,128)S(1)} %shard_map.37) | data formatting | bytes 409600
Async XLA Ops:
  0.0 0.9 %copy-start = (f32[80,640]{1,0:T(8,128)S(1)}, f32[80,640]{1,0:T(8,128)}, u32[]{:S(2)}) copy-start(f32[80,640]{1,0:T(8,128)} %x_ref.1) | copy-start | bytes 614404
  0.9 0.7 %copy-start.1 = (s32[5,5]{1,0:T(8,128)S(1)}, s32[5,5]{1,0:T(8,128)}, u32[]{:S(2)}) copy-start(s32[5,5]{1,0:T(8,128)} %in_ref.1) | copy-start | bytes 304
  1.6 0.7 %copy-start.2 = (s32[5,5]{1,0:T(8,128)S(1)}, s32[5,5]{1,0:T(8,128)}, u32[]{:S(2)}) copy-start(s32[5,5]{1,0:T(8,128)} %out_pat_ref.1) | copy-start | bytes 304

commit v2 on v1

--- a/solution.py
+++ b/solution.py
@@ -20,11 +20,11 @@
 
 
 def kernel(
-    narrow, wide, parts, in_ref, out_pat_ref, x_ref, o_ref,
-    blocks, row_parts, sums, send_sem, recv_sem,
+    narrow, wide, parts, in_hbm, out_hbm, x_hbm, o_ref,
+    in_ref, out_pat_ref, blocks, row_parts, left, total, sums, load_sem, send_sem, recv_sem,
     row_send, row_recv, sum_send, sum_recv,
 ):
-    rows, cols = x_ref.shape
+    rows, cols = x_hbm.shape
     blks = in_ref.shape[0]
     units = cols // LANES
     line = wide // 4
@@ -44,6 +44,15 @@
             SIBLING: (n, index(z, y, 1 - c)),
         }[kind]
 
+    loads = [
+        pltpu.make_async_copy(source, target, load_sem.at[i])
+        for i, (source, target) in enumerate(
+            [(x_hbm, blocks.at[w]), (in_hbm, in_ref), (out_hbm, out_pat_ref)]
+        )
+    ]
+    for load in loads:
+        load.start()
+
     has_up, has_down = z + 1 < line, z >= 1
     others = [lax.rem(n + d, narrow) for d in range(1, narrow)]
 
@@ -75,9 +84,11 @@
             upper, pattern[first, col].astype(jnp.float32), pattern[second, col].astype(jnp.float32)
         )
 
+    for load in loads:
+        load.wait()
     for u in range(units):
         at = slice(u * LANES, (u + 1) * LANES)
-        masked = x_ref[:, at] * keep(in_ref, u)
+        masked = blocks[w, :, at] * keep(in_ref, u)
         blocks[w, :, at] = masked
         row_parts[n, :, at] = masked
 
@@ -127,27 +138,9 @@
             device_id_type=MESH,
         )
 
-    def walk(visit):
-        count = len(parts)
-        for part in range(count):
-            visit(None, w, part, (UP, DOWN, ACROSS, SIBLING), True)
-        across = [p for p in range(count) if parts[p][2]]
-        along = [p for p in range(count) if not parts[p][2]]
-        for part in across:
-            visit(None, index(z, 1 - y, c), part, (UP, DOWN, SIBLING), False)
-        for part in along:
-            visit(None, index(z, 1 - y, c), part, (SIBLING,), False)
-        for step in range(1, line):
-            for part in along:
-                visit(z >= step, index(z - step, y, c), part, (UP, ACROSS, SIBLING), False)
-                visit(z + step < line, index(z + step, y, c), part, (DOWN, ACROSS, SIBLING), False)
-            for part in across:
-                for yy in (y, 1 - y):
-                    visit(z >= step, index(z - step, yy, c), part, (UP, SIBLING), False)
-                    visit(z + step < line, index(z + step, yy, c), part, (DOWN, SIBLING), False)
-            for part in along:
-                visit(z >= step, index(z - step, 1 - y, c), part, (SIBLING,), False)
-                visit(z + step < line, index(z + step, 1 - y, c), part, (SIBLING,), False)
+    count = len(parts)
+    across = [p for p in range(count) if parts[p][2]]
+    along = [p for p in range(count) if not parts[p][2]]
 
     def under(condition, act):
         if condition is None:
@@ -155,36 +148,84 @@
         else:
             pl.when(condition)(act)
 
-    def forward(condition, slot, part, kinds, mine):
+    def own(visit):
+        for part in range(count):
+            visit(None, w, part, (UP, DOWN, ACROSS, SIBLING))
+
+    def beside(visit):
+        for part in across:
+            visit(None, index(z, 1 - y, c), part, (UP, DOWN, SIBLING))
+        for part in along:
+            visit(None, index(z, 1 - y, c), part, (SIBLING,))
+
+    def along_line(step, visit):
+        for part in along:
+            visit(z >= step, index(z - step, y, c), part, (UP, ACROSS, SIBLING))
+            visit(z + step < line, index(z + step, y, c), part, (DOWN, ACROSS, SIBLING))
+
+    def across_line(step, visit):
+        for part in across:
+            for yy in (y, 1 - y):
+                visit(z >= step, index(z - step, yy, c), part, (UP, SIBLING))
+                visit(z + step < line, index(z + step, yy, c), part, (DOWN, SIBLING))
+        for part in along:
+            visit(z >= step, index(z - step, 1 - y, c), part, (SIBLING,))
+            visit(z + step < line, index(z + step, 1 - y, c), part, (SIBLING,))
+
+    def send(condition, slot, part, kinds):
+        under(condition, lambda: [go(kind, slot, part, lambda one: one.start()) for kind in kinds] and None)
+
+    def forward(condition, slot, part, kinds):
         def act():
-            if not mine:
-                arrive(slot, part)
-            for kind in kinds:
-                go(kind, slot, part, lambda one: one.start())
+            arrive(slot, part)
+            send(None, slot, part, kinds)
 
         under(condition, act)
-        if mine and part == len(parts) - 1:
-            for other in others:
-                row_copy(other).start()
-
-    walk(forward)
-    for zz in range(line):
+
+    def drain(condition, slot, part, kinds):
+        under(condition, lambda: [go(kind, slot, part, lambda one: one.wait_send()) for kind in kinds] and None)
+
+    def multiply(plane):
         for yy in range(2):
-            for part in range(len(parts)):
-                arrive(index(zz, yy, 1 - c), part)
-    for other in others:
-        row_arrival(other).wait_recv()
-
-    expanded = None
-    for g in range(narrow):
-        a_high, a_low = split(row_parts[g])
-        both = jnp.concatenate([a_high, a_low], axis=0)
-        b_high, b_low = split(blocks[pl.ds(g * group, group)].reshape(group * rows, cols))
+            for part in range(count):
+                arrive(index(plane, yy, 1 - c), part)
+        b_high, b_low = split(blocks[pl.ds(plane * 4, 4)].reshape(4 * rows, cols))
+        both = left[plane]
         first_two = jnp.dot(both, b_high, preferred_element_type=jnp.float32)
         term = first_two[:rows] + first_two[rows:]
-        term = term + jnp.dot(a_high, b_low, preferred_element_type=jnp.float32)
-        expanded = term if expanded is None else expanded + term
-
+        total[...] += term + jnp.dot(both[:rows], b_low, preferred_element_type=jnp.float32)
+
+    own(send)
+    for other in others:
+        row_copy(other).start()
+    total[...] = jnp.zeros_like(total)
+    beside(forward)
+
+    def prepare():
+        for other in others:
+            row_arrival(other).wait_recv()
+        for g in range(narrow):
+            both = jnp.concatenate(split(row_parts[g]), axis=0)
+            for q in range(group // 4):
+                left[g * (group // 4) + q] = both[:, q * 4 * rows : (q + 1) * 4 * rows]
+
+    def turn(step, carry):
+        along_line(step, forward)
+        pl.when(step == 1)(prepare)
+
+        def one_side(side, carry):
+            plane = z + (2 * side - 1) * (step - 1)
+            live = (plane >= 0) & (plane < line) & ((step > 1) | (side == 0))
+            pl.when(live)(lambda: multiply(plane))
+            return carry
+
+        lax.fori_loop(0, 2, one_side, 0)
+        across_line(step, forward)
+        return carry
+
+    lax.fori_loop(1, line + 1, turn, 0)
+
+    expanded = total[...]
     partial = None
     for u in range(units):
         at = slice(u * LANES, (u + 1) * LANES)
@@ -206,18 +247,23 @@
     for other in others:
         sum_copy(other, n).start()
 
-    def drain(condition, slot, part, kinds, mine):
-        under(condition, lambda: [go(kind, slot, part, lambda one: one.wait_send()) for kind in kinds] and None)
-
-    walk(drain)
+    own(drain)
+    beside(drain)
+
+    def drain_turn(step, carry):
+        along_line(step, drain)
+        across_line(step, drain)
+        return carry
+
+    lax.fori_loop(1, line, drain_turn, 0)
     for other in others:
         row_copy(other).wait_send()
     for other in others:
         sum_copy(other, other).wait_recv()
-    total = sums[0]
+    row_sum = sums[0]
     for g in range(1, narrow):
-        total = total + sums[g]
-    scale = (cols * narrow) / jnp.sum(total, axis=1, keepdims=True)
+        row_sum = row_sum + sums[g]
+    scale = (cols * narrow) / jnp.sum(row_sum, axis=1, keepdims=True)
     o_ref[...] = o_ref[...] * scale
     for other in others:
         sum_copy(other, n).wait_send()
@@ -225,20 +271,25 @@
 
 def body(narrow, wide, state, in_pattern, out_pattern):
     rows, cols = state.shape
-    part = rows // 80 * 64 if rows % 80 == 0 else rows // 2
-    parts = ((0, part, False), (part, rows - part, True))
-    smem = pl.BlockSpec(memory_space=pltpu.SMEM)
+    cut = 2 * rows // 5
+    parts = ((0, cut, False), (cut, cut, False), (2 * cut, rows - 2 * cut, True))
+    hbm = pl.BlockSpec(memory_space=pltpu.HBM)
     vmem = pl.BlockSpec(memory_space=pltpu.VMEM)
     flops = 2 * rows * cols * cols * narrow
     return pl.pallas_call(
         functools.partial(kernel, narrow, wide, parts),
         out_shape=jax.ShapeDtypeStruct((rows, cols), jnp.float32),
-        in_specs=[smem, smem, vmem],
+        in_specs=[hbm, hbm, hbm],
         out_specs=vmem,
         scratch_shapes=[
+            pltpu.SMEM(in_pattern.shape, jnp.int32),
+            pltpu.SMEM(out_pattern.shape, jnp.int32),
             pltpu.VMEM((wide, rows, cols), jnp.float32),
             pltpu.VMEM((narrow, rows, cols), jnp.float32),
+            pltpu.VMEM((wide // 4, 2 * rows, 4 * rows), jnp.bfloat16),
+            pltpu.VMEM((rows, cols), jnp.float32),
             pltpu.VMEM((narrow, rows, LANES), jnp.float32),
+            pltpu.SemaphoreType.DMA((3,)),
             pltpu.SemaphoreType.DMA((4, wide, len(parts))),
             pltpu.SemaphoreType.DMA((wide, len(parts))),
             pltpu.SemaphoreType.DMA((narrow,)),
@@ -247,7 +298,7 @@
             pltpu.SemaphoreType.DMA((narrow,)),
         ],
         compiler_params=pltpu.CompilerParams(
-            collective_id=0, has_side_effects=True, vmem_limit_bytes=48 * 1024 * 1024
+            collective_id=0, has_side_effects=True, vmem_limit_bytes=60 * 1024 * 1024
         ),
         cost_estimate=pl.CostEstimate(flops=flops, bytes_accessed=8 * rows * cols, transcendentals=0),
     )(in_pattern, out_pattern, state)

time: 36.5 us -> 35.3 us (0.967)
  local copies, waits for them, and re-layouts: 2.98 us -> 1.62 us
    unnamed x7 -> x1, local copies, waits for them, and re-layouts: 2.98 us -> 1.62 us
where the time goes in v2:
time: 35.3 us; the launch traced here: 35.2 us
  Pallas kernels  33.5 us (95%)
  local copies, waits for them, and re-layouts  1.62 us (5%)
    pallas_call x1, Pallas kernels, body(): pl.pallas_call(functools.partial(kernel, narrow, wide, parts), out_shape=...  33.5 us
    unnamed x1, local copies, waits for them, and re-layouts  1.62 us

profile of v2, /device:TPU:0, one launch (start us, length us, event | category | flops | bytes accessed | tf_op | source)
XLA Modules:
  0.0 35.2 jit_solution(13664415908780160309)
XLA Ops:
  0.0 33.5 %shard_map.37 = f32[80,640]{1,0:T(8,128)} custom-call(s32[5,5]{1,0:T(8,128)} %in_hbm.1, s32[5,5]{1,0:T(8,128)} %out_hbm.1, f32[80,640]{1,0:T(8,128)} %x_hbm.1), custom_call_target="tpu_custom_call" | custom-call | flops 131072000 | bytes 409600 | tf_op jit(solution)/shard_map/pallas_call | solution.py:279
  33.5 1.6 %copy.5 = f32[80,640]{1,0:T(8,128)} copy(f32[80,640]{1,0:T(8,128)} %shard_map.37) | data formatting | bytes 409600

commit v3 on v2

v3 whole, which is shorter than its diff:
```python
import functools

import jax
import jax.numpy as jnp
from jax import lax
from jax.experimental import pallas as pl
from jax.experimental.pallas import tpu as pltpu
from jax.sharding import PartitionSpec as P

BLK = 256
LANES = 128
MESH = pl.DeviceIdType.MESH
UP, DOWN, ACROSS, SIBLING = range(4)
LINE = UP


def split(value):
    high = value.astype(jnp.bfloat16)
    low = (value - high.astype(jnp.float32)).astype(jnp.bfloat16)
    return high, low


def kernel(
    narrow, wide, cut, in_hbm, out_hbm, x_hbm, o_ref,
    in_ref, out_pat_ref, blocks, row_parts, left, total, sums, load_sem, send_sem, recv_sem,
    row_send, row_recv, sum_send, sum_recv,
):
    rows, cols = x_hbm.shape
    blks = in_ref.shape[0]
    units = cols // LANES
    line = wide // 4
    group = wide // narrow
    n = lax.axis_index("narrow")
    w = lax.axis_index("wide")
    z, y, c = w // 4, (w // 2) % 2, w % 2

    def index(zz, yy, cc):
        return (zz * 2 + yy) * 2 + cc

    def partner(kind):
        return {
            UP: (n, index(z + 1, y, c)),
            DOWN: (n, index(z - 1, y, c)),
            ACROSS: (n, index(z, 1 - y, c)),
            SIBLING: (n, index(z, y, 1 - c)),
        }[kind]

    loads = [
        pltpu.make_async_copy(source, target, load_sem.at[i])
        for i, (source, target) in enumerate(
            [(x_hbm, blocks.at[c, z, y]), (in_hbm, in_ref), (out_hbm, out_pat_ref)]
        )
    ]
    for load in loads:
        load.start()

    has_up, has_down = z + 1 < line, z >= 1
    others = [lax.rem(n + d, narrow) for d in range(1, narrow)]

    barrier = pltpu.get_barrier_semaphore()

    def greet(device):
        pl.semaphore_signal(barrier, inc=1, device_id=device, device_id_type=MESH)

    greet(partner(ACROSS))
    greet(partner(SIBLING))
    for other in others:
        greet((other, w))

    @pl.when(has_up)
    def _():
        greet(partner(UP))

    @pl.when(has_down)
    def _():
        greet(partner(DOWN))

    first = (w * rows) // BLK
    second = jnp.minimum(first + 1, blks - 1)
    upper = lax.broadcasted_iota(jnp.int32, (rows, LANES), 0) < (first + 1) * BLK - w * rows

    def keep(pattern, u):
        col = (n * cols + u * LANES) // BLK
        return jnp.where(
            upper, pattern[first, col].astype(jnp.float32), pattern[second, col].astype(jnp.float32)
        )

    for load in loads:
        load.wait()
    for u in range(units):
        at = slice(u * LANES, (u + 1) * LANES)
        masked = blocks[c, z, y, :, at] * keep(in_ref, u)
        blocks[c, z, y, :, at] = masked
        row_parts[n, :, at] = masked

    met = 1 + 1 + len(others) + has_up.astype(jnp.int32) + has_down.astype(jnp.int32)
    pl.semaphore_wait(barrier, met)

    low, rest = pl.ds(0, 2 * cut), pl.ds(2 * cut, rows - 2 * cut)

    def piece(core, plane, yy, part):
        return blocks.at[core, plane, yy, pl.ds(part * cut, cut), :]

    def both_rest(core, plane):
        return blocks.at[core, plane, :, rest, :]

    def copy(kind, ref, plane, number):
        via = {UP: 0, DOWN: 0, ACROSS: 1, SIBLING: 2}[kind]
        return pltpu.make_async_remote_copy(
            src_ref=ref,
            dst_ref=ref,
            send_sem=send_sem.at[kind, plane, number],
            recv_sem=recv_sem.at[via, plane, number],
            device_id=partner(kind),
            device_id_type=MESH,
        )

    def start(kind, ref, plane, number):
        one = copy(kind, ref, plane, number)
        if kind == UP:
            pl.when(has_up)(one.start)
        elif kind == DOWN:
            pl.when(has_down)(one.start)
        else:
            one.start()

    def finish(kind, ref, plane, number):
        one = copy(kind, ref, plane, number)
        if kind == UP:
            pl.when(has_up)(one.wait_send)
        elif kind == DOWN:
            pl.when(has_down)(one.wait_send)
        else:
            one.wait_send()

    def arrive(kind, ref, plane, number):
        copy(kind, ref, plane, number).wait_recv()

    def nothing(*_):
        pass

    def row_copy(other):
        return pltpu.make_async_remote_copy(
            src_ref=blocks.at[c, z, y],
            dst_ref=row_parts.at[n],
            send_sem=row_send.at[other],
            recv_sem=row_recv.at[n],
            device_id=(other, w),
            device_id_type=MESH,
        )

    def row_arrival(other):
        return pltpu.make_async_remote_copy(
            src_ref=blocks.at[c, z, y],
            dst_ref=row_parts.at[other],
            send_sem=row_send.at[other],
            recv_sem=row_recv.at[other],
            device_id=(other, w),
            device_id_type=MESH,
        )

    def own(act):
        for part in range(2):
            ref = piece(c, z, y, part)
            for kind in (UP, DOWN, ACROSS):
                act(kind, ref, z, part)
        act(ACROSS, blocks.at[c, z, y, rest, :], z, 2)
        act(SIBLING, blocks.at[c, z, y, low, :], z, 0)

    def beside(wait, act):
        wait(ACROSS, blocks.at[c, z, 1 - y, rest, :], z, 2)
        for kind in (UP, DOWN, SIBLING):
            act(kind, both_rest(c, z), z, 2)
        from_across(z, wait, act)

    def from_across(plane, wait, act):
        for part in range(2):
            wait(ACROSS, piece(c, plane, 1 - y, part), plane, part)
        act(SIBLING, blocks.at[c, plane, 1 - y, low, :], plane, 1)

    def sides(step, visit):
        pl.when(z >= step)(lambda: visit(z - step, UP))
        pl.when(z + step < line)(lambda: visit(z + step, DOWN))

    def along_line(step, wait, act):
        for part in range(2):

            def one_piece(plane, kind):
                ref = piece(c, plane, y, part)
                wait(LINE, ref, plane, part)
                act(kind, ref, plane, part)
                act(ACROSS, ref, plane, part)
                if part == 1:
                    act(SIBLING, blocks.at[c, plane, y, low, :], plane, 0)

            sides(step, one_piece)

    def rest_of_line(step, wait, act):
        def the_rest(plane, kind):
            ref = both_rest(c, plane)
            wait(LINE, ref, plane, 2)
            act(kind, ref, plane, 2)
            act(SIBLING, ref, plane, 2)

        sides(step, the_rest)
        sides(step, lambda plane, kind: from_across(plane, wait, act))

    def half(plane, core):
        b_high, b_low = split(blocks[core, plane].reshape(2 * rows, cols))
        pair = left[plane, core]
        first_two = jnp.dot(pair, b_high, preferred_element_type=jnp.float32)
        term = first_two[:rows] + first_two[rows:]
        total[...] += term + jnp.dot(pair[:rows], b_low, preferred_element_type=jnp.float32)

    def multiply(plane):
        def one_half(h, carry):
            @pl.when(h == 1)
            def _():
                arrive(SIBLING, blocks.at[1 - c, plane, y, low, :], plane, 0)
                arrive(SIBLING, blocks.at[1 - c, plane, 1 - y, low, :], plane, 1)
                arrive(SIBLING, both_rest(1 - c, plane), plane, 2)

            half(plane, (c + h) % 2)
            return carry

        lax.fori_loop(0, 2, one_half, 0)

    own(start)
    for other in others:
        row_copy(other).start()
    total[...] = jnp.zeros_like(total)
    beside(arrive, start)

    def prepare():
        for other in others:
            row_arrival(other).wait_recv()
        for g in range(narrow):
            both = jnp.concatenate(split(row_parts[g]), axis=0)
            for q in range(group // 4):
                for core in range(2):
                    begins = [(q * 4 + 2 * yy + core) * rows for yy in range(2)]
                    left[g * (group // 4) + q, core] = jnp.concatenate(
                        [both[:, begin : begin + rows] for begin in begins], axis=1
                    )

    def turn(step, carry):
        along_line(step, arrive, start)
        pl.when(step == 1)(prepare)

        def one_side(side, carry):
            plane = z + (2 * side - 1) * (step - 1)
            live = (plane >= 0) & (plane < line) & ((step > 1) | (side == 0))
            pl.when(live)(lambda: multiply(plane))
            return carry

        lax.fori_loop(0, 2, one_side, 0)
        rest_of_line(step, arrive, start)
        return carry

    lax.fori_loop(1, line + 1, turn, 0)

    expanded = total[...]
    partial = None
    for u in range(units):
        at = slice(u * LANES, (u + 1) * LANES)
        inflated = expanded[:, at] * expanded[:, at] * keep(out_pat_ref, u)
        o_ref[:, at] = inflated
        partial = inflated if partial is None else partial + inflated
    sums[n] = partial

    def sum_copy(other, slot):
        return pltpu.make_async_remote_copy(
            src_ref=sums.at[n],
            dst_ref=sums.at[slot],
            send_sem=sum_send.at[other],
            recv_sem=sum_recv.at[slot],
            device_id=(other, w),
            device_id_type=MESH,
        )

    for other in others:
        sum_copy(other, n).start()

    own(finish)
    beside(nothing, finish)

    def drain_turn(step, carry):
        along_line(step, nothing, finish)
        rest_of_line(step, nothing, finish)
        return carry

    lax.fori_loop(1, line, drain_turn, 0)
    for other in others:
        row_copy(other).wait_send()
    for other in others:
        sum_copy(other, other).wait_recv()
    row_sum = sums[0]
    for g in range(1, narrow):
        row_sum = row_sum + sums[g]
    scale = (cols * narrow) / jnp.sum(row_sum, axis=1, keepdims=True)
    o_ref[...] = o_ref[...] * scale
    for other in others:
        sum_copy(other, n).wait_send()


def body(narrow, wide, state, in_pattern, out_pattern):
    rows, cols = state.shape
    cut = 2 * rows // 5
    line = wide // 4
    hbm = pl.BlockSpec(memory_space=pltpu.HBM)
    vmem = pl.BlockSpec(memory_space=pltpu.VMEM)
    flops = 2 * rows * cols * cols * narrow
    return pl.pallas_call(
        functools.partial(kernel, narrow, wide, cut),
        out_shape=pltpu.VMEM((rows, cols), jnp.float32),
        in_specs=[hbm, hbm, hbm],
        out_specs=vmem,
        scratch_shapes=[
            pltpu.SMEM(in_pattern.shape, jnp.int32),
            pltpu.SMEM(out_pattern.shape, jnp.int32),
            pltpu.VMEM((2, line, 2, rows, cols), jnp.float32),
            pltpu.VMEM((narrow, rows, cols), jnp.float32),
            pltpu.VMEM((line, 2, 2 * rows, 2 * rows), jnp.bfloat16),
            pltpu.VMEM((rows, cols), jnp.float32),
            pltpu.VMEM((narrow, rows, LANES), jnp.float32),
            pltpu.SemaphoreType.DMA((3,)),
            pltpu.SemaphoreType.DMA((4, line, 3)),
            pltpu.SemaphoreType.DMA((3, line, 3)),
            pltpu.SemaphoreType.DMA((narrow,)),
            pltpu.SemaphoreType.DMA((narrow,)),
            pltpu.SemaphoreType.DMA((narrow,)),
            pltpu.SemaphoreType.DMA((narrow,)),
        ],
        compiler_params=pltpu.CompilerParams(
            collective_id=0, has_side_effects=True, vmem_limit_bytes=48 * 1024 * 1024
        ),
        cost_estimate=pl.CostEstimate(flops=flops, bytes_accessed=8 * rows * cols, transcendentals=0),
    )(*[pltpu.with_memory_space_constraint(a, pltpu.HBM) for a in (in_pattern, out_pattern, state)])


def solution(mesh):
    return jax.shard_map(
        functools.partial(body, mesh.shape["narrow"], mesh.shape["wide"]),
        mesh=mesh,
        in_specs=(P("wide", "narrow"), P(), P()),
        out_specs=P("wide", "narrow"),
        check_vma=False,
    )
```

time: 35.3 us -> 32.4 us (0.918)
  Pallas kernels: 33.5 us -> 31.5 us
  local copies, waits for them, and re-layouts: 1.62 us -> 0.68 us
    pallas_call x1, Pallas kernels: 33.5 us -> 31.5 us  [body(): pl.pallas_call(functools.partial(kernel, narrow, wide, cut), out_shape=pl...]
    unnamed x1, local copies, waits for them, and re-layouts: 1.62 us -> 0.68 us
where the time goes in v3:
time: 32.4 us; the launch traced here: 32.2 us
  Pallas kernels  31.5 us (97%)
  local copies, waits for them, and re-layouts  0.68 us (2%)
    pallas_call x1, Pallas kernels, body(): pl.pallas_call(functools.partial(kernel, narrow, wide, cut), out_shape=pl...  31.5 us
    unnamed x1, local copies, waits for them, and re-layouts  0.68 us

profile of v3, /device:TPU:0, one launch (start us, length us, event | category | flops | bytes accessed | tf_op | source)
XLA Modules:
  0.0 32.2 jit_solution(3704838365931416103)
XLA Ops:
  0.0 31.5 %shard_map.37 = f32[80,640]{1,0:T(8,128)S(1)} custom-call(s32[5,5]{1,0:T(8,128)} %in_hbm.1, s32[5,5]{1,0:T(8,128)} %out_hbm.1, f32[80,640]{1,0:T(8,128)} %x_hbm.1), custom_call_target="tpu_custom_call" | custom-call | flops 131072000 | bytes 409600 | tf_op jit(solution)/shard_map/pallas_call | solution.py:313
  31.5 0.7 %copy.5 = f32[80,640]{1,0:T(8,128)} copy(f32[80,640]{1,0:T(8,128)S(1)} %shard_map.37) | data formatting | bytes 409600

commit v4 on v3

--- a/solution.py
+++ b/solution.py
@@ -160,18 +160,17 @@
         )
 
     def own(act):
+        act(ACROSS, blocks.at[c, z, y, rest, :], z, 2)
         for part in range(2):
             ref = piece(c, z, y, part)
             for kind in (UP, DOWN, ACROSS):
                 act(kind, ref, z, part)
-        act(ACROSS, blocks.at[c, z, y, rest, :], z, 2)
         act(SIBLING, blocks.at[c, z, y, low, :], z, 0)
 
     def beside(wait, act):
         wait(ACROSS, blocks.at[c, z, 1 - y, rest, :], z, 2)
         for kind in (UP, DOWN, SIBLING):
             act(kind, both_rest(c, z), z, 2)
-        from_across(z, wait, act)
 
     def from_across(plane, wait, act):
         for part in range(2):
@@ -245,7 +244,11 @@
 
     def turn(step, carry):
         along_line(step, arrive, start)
-        pl.when(step == 1)(prepare)
+
+        @pl.when(step == 1)
+        def _():
+            from_across(z, arrive, start)
+            prepare()
 
         def one_side(side, carry):
             plane = z + (2 * side - 1) * (step - 1)
@@ -283,6 +286,7 @@
 
     own(finish)
     beside(nothing, finish)
+    from_across(z, nothing, finish)
 
     def drain_turn(step, carry):
         along_line(step, nothing, finish)

time: 32.4 us -> 30.8 us (0.951)
  Pallas kernels: 31.5 us -> 30 us
    pallas_call x1, Pallas kernels: 31.5 us -> 30 us  [body(): pl.pallas_call(functools.partial(kernel, narrow, wide, cut), out_shape=pl...]
where the time goes in v4:
time: 30.8 us; the launch traced here: 30.7 us
  Pallas kernels  30 us (97%)
  local copies, waits for them, and re-layouts  0.68 us (2%)
    pallas_call x1, Pallas kernels, body(): pl.pallas_call(functools.partial(kernel, narrow, wide, cut), out_shape=pl...  30 us
    unnamed x1, local copies, waits for them, and re-layouts  0.68 us

profile of v4, /device:TPU:0, one launch (start us, length us, event | category | flops | bytes accessed | tf_op | source)
XLA Modules:
  0.0 30.7 jit_solution(18197880904736552581)
XLA Ops:
  0.0 30.0 %shard_map.37 = f32[80,640]{1,0:T(8,128)S(1)} custom-call(s32[5,5]{1,0:T(8,128)} %in_hbm.1, s32[5,5]{1,0:T(8,128)} %out_hbm.1, f32[80,640]{1,0:T(8,128)} %x_hbm.1), custom_call_target="tpu_custom_call" | custom-call | flops 131072000 | bytes 409600 | tf_op jit(solution)/shard_map/pallas_call | solution.py:317
  30.0 0.7 %copy.5 = f32[80,640]{1,0:T(8,128)} copy(f32[80,640]{1,0:T(8,128)S(1)} %shard_map.37) | data formatting | bytes 409600

commit v5 on v4

--- a/solution.py
+++ b/solution.py
@@ -202,7 +202,6 @@
             act(SIBLING, ref, plane, 2)
 
         sides(step, the_rest)
-        sides(step, lambda plane, kind: from_across(plane, wait, act))
 
     def half(plane, core):
         b_high, b_low = split(blocks[core, plane].reshape(2 * rows, cols))
@@ -242,22 +241,31 @@
                         [both[:, begin : begin + rows] for begin in begins], axis=1
                     )
 
-    def turn(step, carry):
-        along_line(step, arrive, start)
-
-        @pl.when(step == 1)
+    def late(step):
+        @pl.when(step == 0)
         def _():
             from_across(z, arrive, start)
             prepare()
 
+        @pl.when(step > 0)
+        def _():
+            sides(step, lambda plane, kind: from_across(plane, arrive, start))
+
         def one_side(side, carry):
-            plane = z + (2 * side - 1) * (step - 1)
-            live = (plane >= 0) & (plane < line) & ((step > 1) | (side == 0))
+            plane = z + (2 * side - 1) * step
+            live = (plane >= 0) & (plane < line) & ((step > 0) | (side == 0))
             pl.when(live)(lambda: multiply(plane))
             return carry
 
         lax.fori_loop(0, 2, one_side, 0)
+
+    at_end = (z == 0) | (z == line - 1)
+
+    def turn(step, carry):
+        along_line(step, arrive, start)
+        pl.when(at_end)(lambda: late(step - 1))
         rest_of_line(step, arrive, start)
+        pl.when(jnp.logical_not(at_end))(lambda: late(step - 1))
         return carry
 
     lax.fori_loop(1, line + 1, turn, 0)
@@ -291,6 +299,7 @@
     def drain_turn(step, carry):
         along_line(step, nothing, finish)
         rest_of_line(step, nothing, finish)
+        sides(step, lambda plane, kind: from_across(plane, nothing, finish))
         return carry
 
     lax.fori_loop(1, line, drain_turn, 0)

time: 30.8 us -> 29.5 us (0.958)
  Pallas kernels: 30 us -> 28.7 us
    pallas_call x1, Pallas kernels: 30 us -> 28.7 us  [body(): pl.pallas_call(functools.partial(kernel, narrow, wide, cut), out_shape=pl...]
where the time goes in v5:
time: 29.5 us; the launch traced here: 29.4 us
  Pallas kernels  28.7 us (97%)
  local copies, waits for them, and re-layouts  0.68 us (2%)
    pallas_call x1, Pallas kernels, body(): pl.pallas_call(functools.partial(kernel, narrow, wide, cut), out_shape=pl...  28.7 us
    unnamed x1, local copies, waits for them, and re-layouts  0.68 us

profile of v5, /device:TPU:0, one launch (start us, length us, event | category | flops | bytes accessed | tf_op | source)
XLA Modules:
  0.0 29.4 jit_solution(18171023408024020502)
XLA Ops:
  0.0 28.7 %shard_map.37 = f32[80,640]{1,0:T(8,128)S(1)} custom-call(s32[5,5]{1,0:T(8,128)} %in_hbm.1, s32[5,5]{1,0:T(8,128)} %out_hbm.1, f32[80,640]{1,0:T(8,128)} %x_hbm.1), custom_call_target="tpu_custom_call" | custom-call | flops 131072000 | bytes 409600 | tf_op jit(solution)/shard_map/pallas_call | solution.py:326
  28.7 0.7 %copy.5 = f32[80,640]{1,0:T(8,128)} copy(f32[80,640]{1,0:T(8,128)S(1)} %shard_map.37) | data formatting | bytes 409600

commit v6 on v5

--- a/solution.py
+++ b/solution.py
@@ -48,7 +48,12 @@
     loads = [
         pltpu.make_async_copy(source, target, load_sem.at[i])
         for i, (source, target) in enumerate(
-            [(x_hbm, blocks.at[c, z, y]), (in_hbm, in_ref), (out_hbm, out_pat_ref)]
+            [
+                (x_hbm, blocks.at[c, z, y]),
+                (x_hbm, row_parts.at[n]),
+                (in_hbm, in_ref),
+                (out_hbm, out_pat_ref),
+            ]
         )
     ]
     for load in loads:
@@ -75,23 +80,17 @@
     def _():
         greet(partner(DOWN))
 
-    first = (w * rows) // BLK
-    second = jnp.minimum(first + 1, blks - 1)
-    upper = lax.broadcasted_iota(jnp.int32, (rows, LANES), 0) < (first + 1) * BLK - w * rows
-
-    def keep(pattern, u):
-        col = (n * cols + u * LANES) // BLK
+    def keep(pattern, shard, part, u):
+        first = (shard * rows) // BLK
+        second = jnp.minimum(first + 1, blks - 1)
+        col = (part * cols + u * LANES) // BLK
+        upper = lax.broadcasted_iota(jnp.int32, (rows, LANES), 0) < (first + 1) * BLK - shard * rows
         return jnp.where(
             upper, pattern[first, col].astype(jnp.float32), pattern[second, col].astype(jnp.float32)
         )
 
-    for load in loads:
-        load.wait()
-    for u in range(units):
-        at = slice(u * LANES, (u + 1) * LANES)
-        masked = blocks[c, z, y, :, at] * keep(in_ref, u)
-        blocks[c, z, y, :, at] = masked
-        row_parts[n, :, at] = masked
+    def keep_all(shard, part):
+        return jnp.concatenate([keep(in_ref, shard, part, u) for u in range(units)], axis=1)
 
     met = 1 + 1 + len(others) + has_up.astype(jnp.int32) + has_down.astype(jnp.int32)
     pl.semaphore_wait(barrier, met)
@@ -104,10 +103,10 @@
     def both_rest(core, plane):
         return blocks.at[core, plane, :, rest, :]
 
-    def copy(kind, ref, plane, number):
+    def copy(kind, ref, plane, number, source=None):
         via = {UP: 0, DOWN: 0, ACROSS: 1, SIBLING: 2}[kind]
         return pltpu.make_async_remote_copy(
-            src_ref=ref,
+            src_ref=ref if source is None else source,
             dst_ref=ref,
             send_sem=send_sem.at[kind, plane, number],
             recv_sem=recv_sem.at[via, plane, number],
@@ -115,8 +114,8 @@
             device_id_type=MESH,
         )
 
-    def start(kind, ref, plane, number):
-        one = copy(kind, ref, plane, number)
+    def start(kind, ref, plane, number, source=None):
+        one = copy(kind, ref, plane, number, source)
         if kind == UP:
             pl.when(has_up)(one.start)
         elif kind == DOWN:
@@ -124,8 +123,8 @@
         else:
             one.start()
 
-    def finish(kind, ref, plane, number):
-        one = copy(kind, ref, plane, number)
+    def finish(kind, ref, plane, number, source=None):
+        one = copy(kind, ref, plane, number, source)
         if kind == UP:
             pl.when(has_up)(one.wait_send)
         elif kind == DOWN:
@@ -141,7 +140,7 @@
 
     def row_copy(other):
         return pltpu.make_async_remote_copy(
-            src_ref=blocks.at[c, z, y],
+            src_ref=x_hbm,
             dst_ref=row_parts.at[n],
             send_sem=row_send.at[other],
             recv_sem=row_recv.at[n],
@@ -151,7 +150,7 @@
 
     def row_arrival(other):
         return pltpu.make_async_remote_copy(
-            src_ref=blocks.at[c, z, y],
+            src_ref=x_hbm,
             dst_ref=row_parts.at[other],
             send_sem=row_send.at[other],
             recv_sem=row_recv.at[other],
@@ -160,12 +159,12 @@
         )
 
     def own(act):
-        act(ACROSS, blocks.at[c, z, y, rest, :], z, 2)
+        act(ACROSS, blocks.at[c, z, y, rest, :], z, 2, x_hbm.at[rest, :])
         for part in range(2):
             ref = piece(c, z, y, part)
             for kind in (UP, DOWN, ACROSS):
-                act(kind, ref, z, part)
-        act(SIBLING, blocks.at[c, z, y, low, :], z, 0)
+                act(kind, ref, z, part, x_hbm.at[pl.ds(part * cut, cut), :])
+        act(SIBLING, blocks.at[c, z, y, low, :], z, 0, x_hbm.at[low, :])
 
     def beside(wait, act):
         wait(ACROSS, blocks.at[c, z, 1 - y, rest, :], z, 2)
@@ -204,7 +203,8 @@
         sides(step, the_rest)
 
     def half(plane, core):
-        b_high, b_low = split(blocks[core, plane].reshape(2 * rows, cols))
+        masked = [blocks[core, plane, yy] * keep_all(index(plane, yy, core), n) for yy in range(2)]
+        b_high, b_low = split(jnp.concatenate(masked, axis=0))
         pair = left[plane, core]
         first_two = jnp.dot(pair, b_high, preferred_element_type=jnp.float32)
         term = first_two[:rows] + first_two[rows:]
@@ -227,13 +227,15 @@
     for other in others:
         row_copy(other).start()
     total[...] = jnp.zeros_like(total)
+    for load in loads:
+        load.wait()
     beside(arrive, start)
 
     def prepare():
         for other in others:
             row_arrival(other).wait_recv()
         for g in range(narrow):
-            both = jnp.concatenate(split(row_parts[g]), axis=0)
+            both = jnp.concatenate(split(row_parts[g] * keep_all(w, g)), axis=0)
             for q in range(group // 4):
                 for core in range(2):
                     begins = [(q * 4 + 2 * yy + core) * rows for yy in range(2)]
@@ -274,7 +276,7 @@
     partial = None
     for u in range(units):
         at = slice(u * LANES, (u + 1) * LANES)
-        inflated = expanded[:, at] * expanded[:, at] * keep(out_pat_ref, u)
+        inflated = expanded[:, at] * expanded[:, at] * keep(out_pat_ref, w, n, u)
         o_ref[:, at] = inflated
         partial = inflated if partial is None else partial + inflated
     sums[n] = partial
@@ -336,7 +338,7 @@
             pltpu.VMEM((line, 2, 2 * rows, 2 * rows), jnp.bfloat16),
             pltpu.VMEM((rows, cols), jnp.float32),
             pltpu.VMEM((narrow, rows, LANES), jnp.float32),
-            pltpu.SemaphoreType.DMA((3,)),
+            pltpu.SemaphoreType.DMA((4,)),
             pltpu.SemaphoreType.DMA((4, line, 3)),
             pltpu.SemaphoreType.DMA((3, line, 3)),
             pltpu.SemaphoreType.DMA((narrow,)),

time: 29.5 us -> 30 us (1.017)
  Pallas kernels: 28.7 us -> 29.2 us
    pallas_call x1, Pallas kernels: 28.7 us -> 29.2 us  [body(): pl.pallas_call(functools.partial(kernel, narrow, wide, cut), out_shape=pl...]
where the time goes in v6:
time: 30 us; the launch traced here: 29.9 us
  Pallas kernels  29.2 us (97%)
  local copies, waits for them, and re-layouts  0.68 us (2%)
    pallas_call x1, Pallas kernels, body(): pl.pallas_call(functools.partial(kernel, narrow, wide, cut), out_shape=pl...  29.2 us
    unnamed x1, local copies, waits for them, and re-layouts  0.68 us

profile of v6, /device:TPU:0, one launch (start us, length us, event | category | flops | bytes accessed | tf_op | source)
XLA Modules:
  0.0 29.9 jit_solution(18192338182358465819)
XLA Ops:
  0.0 29.2 %shard_map.37 = f32[80,640]{1,0:T(8,128)S(1)} custom-call(s32[5,5]{1,0:T(8,128)} %in_hbm.1, s32[5,5]{1,0:T(8,128)} %out_hbm.1, f32[80,640]{1,0:T(8,128)} %x_hbm.1), custom_call_target="tpu_custom_call" | custom-call | flops 131072000 | bytes 409600 | tf_op jit(solution)/shard_map/pallas_call | solution.py:328
  29.2 0.7 %copy.5 = f32[80,640]{1,0:T(8,128)} copy(f32[80,640]{1,0:T(8,128)S(1)} %shard_map.37) | data formatting | bytes 409600

commit v7 on v5

--- a/solution.py
+++ b/solution.py
@@ -96,10 +96,10 @@
     met = 1 + 1 + len(others) + has_up.astype(jnp.int32) + has_down.astype(jnp.int32)
     pl.semaphore_wait(barrier, met)
 
-    low, rest = pl.ds(0, 2 * cut), pl.ds(2 * cut, rows - 2 * cut)
+    low, rest = pl.ds(0, cut[1]), pl.ds(cut[1], rows - cut[1])
 
     def piece(core, plane, yy, part):
-        return blocks.at[core, plane, yy, pl.ds(part * cut, cut), :]
+        return blocks.at[core, plane, yy, pl.ds((0, cut[0])[part], (cut[0], cut[1] - cut[0])[part]), :]
 
     def both_rest(core, plane):
         return blocks.at[core, plane, :, rest, :]
@@ -318,7 +318,7 @@
 
 def body(narrow, wide, state, in_pattern, out_pattern):
     rows, cols = state.shape
-    cut = 2 * rows // 5
+    cut = (rows // 2, 9 * rows // 10)
     line = wide // 4
     hbm = pl.BlockSpec(memory_space=pltpu.HBM)
     vmem = pl.BlockSpec(memory_space=pltpu.VMEM)

time: 29.5 us -> 29.4 us (level)
  no operation moved by 1% of the time
where the time goes in v7:
time: 29.4 us; the launch traced here: 29.2 us
  Pallas kernels  28.5 us (97%)
  local copies, waits for them, and re-layouts  0.68 us (2%)
    pallas_call x1, Pallas kernels, body(): pl.pallas_call(functools.partial(kernel, narrow, wide, cut), out_shape=pl...  28.5 us
    unnamed x1, local copies, waits for them, and re-layouts  0.68 us

profile of v7, /device:TPU:0, one launch (start us, length us, event | category | flops | bytes accessed | tf_op | source)
XLA Modules:
  0.0 29.2 jit_solution(13132546784168253140)
XLA Ops:
  0.0 28.5 %shard_map.37 = f32[80,640]{1,0:T(8,128)S(1)} custom-call(s32[5,5]{1,0:T(8,128)} %in_hbm.1, s32[5,5]{1,0:T(8,128)} %out_hbm.1, f32[80,640]{1,0:T(8,128)} %x_hbm.1), custom_call_target="tpu_custom_call" | custom-call | flops 131072000 | bytes 409600 | tf_op jit(solution)/shard_map/pallas_call | solution.py:326
  28.5 0.7 %copy.5 = f32[80,640]{1,0:T(8,128)} copy(f32[80,640]{1,0:T(8,128)S(1)} %shard_map.37) | data formatting | bytes 409600

commit v8 on v5

--- a/solution.py
+++ b/solution.py
@@ -261,7 +261,19 @@
 
     at_end = (z == 0) | (z == line - 1)
 
+    def drain_line(step, carry):
+        along_line(step, nothing, finish)
+        rest_of_line(step, nothing, finish)
+        return carry
+
     def turn(step, carry):
+        @pl.when(step == line - 1)
+        def _():
+            own(finish)
+            beside(nothing, finish)
+            from_across(z, nothing, finish)
+            lax.fori_loop(1, line - 2, drain_line, 0)
+
         along_line(step, arrive, start)
         pl.when(at_end)(lambda: late(step - 1))
         rest_of_line(step, arrive, start)
@@ -277,7 +289,9 @@
         inflated = expanded[:, at] * expanded[:, at] * keep(out_pat_ref, u)
         o_ref[:, at] = inflated
         partial = inflated if partial is None else partial + inflated
-    sums[n] = partial
+    wide_sums = jnp.broadcast_to(jnp.sum(partial, axis=1, keepdims=True), (rows, LANES))
+    padded = jnp.concatenate([wide_sums, jnp.ones((LANES - rows, LANES), jnp.float32)], axis=0)
+    sums[n] = padded.T[:8]
 
     def sum_copy(other, slot):
         return pltpu.make_async_remote_copy(
@@ -292,17 +306,12 @@
     for other in others:
         sum_copy(other, n).start()
 
-    own(finish)
-    beside(nothing, finish)
-    from_across(z, nothing, finish)
-
-    def drain_turn(step, carry):
-        along_line(step, nothing, finish)
-        rest_of_line(step, nothing, finish)
+    def drain_across(step, carry):
         sides(step, lambda plane, kind: from_across(plane, nothing, finish))
         return carry
 
-    lax.fori_loop(1, line, drain_turn, 0)
+    lax.fori_loop(line - 2, line, drain_line, 0)
+    lax.fori_loop(1, line, drain_across, 0)
     for other in others:
         row_copy(other).wait_send()
     for other in others:
@@ -310,8 +319,11 @@
     row_sum = sums[0]
     for g in range(1, narrow):
         row_sum = row_sum + sums[g]
-    scale = (cols * narrow) / jnp.sum(row_sum, axis=1, keepdims=True)
-    o_ref[...] = o_ref[...] * scale
+    spread = jnp.broadcast_to(row_sum[:1], (LANES, LANES)).T[:rows]
+    scale = (cols * narrow) / spread
+    for u in range(units):
+        at = slice(u * LANES, (u + 1) * LANES)
+        o_ref[:, at] = o_ref[:, at] * scale
     for other in others:
         sum_copy(other, n).wait_send()
 
@@ -335,7 +347,7 @@
             pltpu.VMEM((narrow, rows, cols), jnp.float32),
             pltpu.VMEM((line, 2, 2 * rows, 2 * rows), jnp.bfloat16),
             pltpu.VMEM((rows, cols), jnp.float32),
-            pltpu.VMEM((narrow, rows, LANES), jnp.float32),
+            pltpu.VMEM((narrow, 8, LANES), jnp.float32),
             pltpu.SemaphoreType.DMA((3,)),
             pltpu.SemaphoreType.DMA((4, line, 3)),
             pltpu.SemaphoreType.DMA((3, line, 3)),

time: 29.5 us -> 29.2 us (0.990)
  Pallas kernels: 28.7 us -> 28.4 us
where the time goes in v8:
time: 29.2 us; the launch traced here: 29.1 us
  Pallas kernels  28.4 us (97%)
  local copies, waits for them, and re-layouts  0.68 us (2%)
    pallas_call x1, Pallas kernels, body(): pl.pallas_call(functools.partial(kernel, narrow, wide, cut), out_shape=pl...  28.4 us
    unnamed x1, local copies, waits for them, and re-layouts  0.68 us

profile of v8, /device:TPU:0, one launch (start us, length us, event | category | flops | bytes accessed | tf_op | source)
XLA Modules:
  0.0 29.1 jit_solution(7214720555971245856)
XLA Ops:
  0.0 28.4 %shard_map.37 = f32[80,640]{1,0:T(8,128)S(1)} custom-call(s32[5,5]{1,0:T(8,128)} %in_hbm.1, s32[5,5]{1,0:T(8,128)} %out_hbm.1, f32[80,640]{1,0:T(8,128)} %x_hbm.1), custom_call_target="tpu_custom_call" | custom-call | flops 131072000 | bytes 409600 | tf_op jit(solution)/shard_map/pallas_call | solution.py:338
  28.4 0.7 %copy.5 = f32[80,640]{1,0:T(8,128)} copy(f32[80,640]{1,0:T(8,128)S(1)} %shard_map.37) | data formatting | bytes 409600

commit v9 on v8

--- a/solution.py
+++ b/solution.py
@@ -181,8 +181,10 @@
         pl.when(z >= step)(lambda: visit(z - step, UP))
         pl.when(z + step < line)(lambda: visit(z + step, DOWN))
 
-    def along_line(step, wait, act):
+    def along_line(step, wait, act, between=None):
         for part in range(2):
+            if part == 1 and between is not None:
+                between()
 
             def one_piece(plane, kind):
                 ref = piece(c, plane, y, part)
@@ -241,15 +243,16 @@
                         [both[:, begin : begin + rows] for begin in begins], axis=1
                     )
 
+    def take_across(step):
+        pl.when(step == 0)(lambda: from_across(z, arrive, start))
+        pl.when(step > 0)(
+            lambda: sides(step, lambda plane, kind: from_across(plane, arrive, start))
+        )
+
     def late(step):
         @pl.when(step == 0)
         def _():
-            from_across(z, arrive, start)
             prepare()
-
-        @pl.when(step > 0)
-        def _():
-            sides(step, lambda plane, kind: from_across(plane, arrive, start))
 
         def one_side(side, carry):
             plane = z + (2 * side - 1) * step
@@ -274,10 +277,19 @@
             from_across(z, nothing, finish)
             lax.fori_loop(1, line - 2, drain_line, 0)
 
-        along_line(step, arrive, start)
+        early = at_end & (step > 1)
+        along_line(
+            step, arrive, start, lambda: pl.when(early)(lambda: take_across(step - 1))
+        )
+        pl.when(jnp.logical_not(early) & at_end)(lambda: take_across(step - 1))
         pl.when(at_end)(lambda: late(step - 1))
         rest_of_line(step, arrive, start)
-        pl.when(jnp.logical_not(at_end))(lambda: late(step - 1))
+
+        @pl.when(jnp.logical_not(at_end))
+        def _():
+            take_across(step - 1)
+            late(step - 1)
+
         return carry
 
     lax.fori_loop(1, line + 1, turn, 0)

time: 29.2 us -> 29.2 us (level)
  no operation moved by 1% of the time
where the time goes in v9:
time: 29.2 us; the launch traced here: 29.1 us
  Pallas kernels  28.4 us (97%)
  local copies, waits for them, and re-layouts  0.68 us (2%)
    pallas_call x1, Pallas kernels, body(): pl.pallas_call(functools.partial(kernel, narrow, wide, cut), out_shape=pl...  28.4 us
    unnamed x1, local copies, waits for them, and re-layouts  0.68 us

profile of v9, /device:TPU:0, one launch (start us, length us, event | category | flops | bytes accessed | tf_op | source)
XLA Modules:
  0.0 29.1 jit_solution(14255191498777068568)
XLA Ops:
  0.0 28.4 %shard_map.37 = f32[80,640]{1,0:T(8,128)S(1)} custom-call(s32[5,5]{1,0:T(8,128)} %in_hbm.1, s32[5,5]{1,0:T(8,128)} %out_hbm.1, f32[80,640]{1,0:T(8,128)} %x_hbm.1), custom_call_target="tpu_custom_call" | custom-call | flops 131072000 | bytes 409600 | tf_op jit(solution)/shard_map/pallas_call | solution.py:350
  28.4 0.7 %copy.5 = f32[80,640]{1,0:T(8,128)} copy(f32[80,640]{1,0:T(8,128)S(1)} %shard_map.37) | data formatting | bytes 409600

commit v10 on v8

--- a/solution.py
+++ b/solution.py
@@ -29,6 +29,7 @@
     blks = in_ref.shape[0]
     units = cols // LANES
     line = wide // 4
+    pieces = len(cut) - 1
     group = wide // narrow
     n = lax.axis_index("narrow")
     w = lax.axis_index("wide")
@@ -96,10 +97,10 @@
     met = 1 + 1 + len(others) + has_up.astype(jnp.int32) + has_down.astype(jnp.int32)
     pl.semaphore_wait(barrier, met)
 
-    low, rest = pl.ds(0, 2 * cut), pl.ds(2 * cut, rows - 2 * cut)
+    low, rest = pl.ds(0, cut[-1]), pl.ds(cut[-1], rows - cut[-1])
 
     def piece(core, plane, yy, part):
-        return blocks.at[core, plane, yy, pl.ds(part * cut, cut), :]
+        return blocks.at[core, plane, yy, pl.ds(cut[part], cut[part + 1] - cut[part]), :]
 
     def both_rest(core, plane):
         return blocks.at[core, plane, :, rest, :]
@@ -160,20 +161,20 @@
         )
 
     def own(act):
-        act(ACROSS, blocks.at[c, z, y, rest, :], z, 2)
-        for part in range(2):
+        act(ACROSS, blocks.at[c, z, y, rest, :], z, pieces)
+        for part in range(pieces):
             ref = piece(c, z, y, part)
             for kind in (UP, DOWN, ACROSS):
                 act(kind, ref, z, part)
         act(SIBLING, blocks.at[c, z, y, low, :], z, 0)
 
     def beside(wait, act):
-        wait(ACROSS, blocks.at[c, z, 1 - y, rest, :], z, 2)
+        wait(ACROSS, blocks.at[c, z, 1 - y, rest, :], z, pieces)
         for kind in (UP, DOWN, SIBLING):
-            act(kind, both_rest(c, z), z, 2)
+            act(kind, both_rest(c, z), z, pieces)
 
     def from_across(plane, wait, act):
-        for part in range(2):
+        for part in range(pieces):
             wait(ACROSS, piece(c, plane, 1 - y, part), plane, part)
         act(SIBLING, blocks.at[c, plane, 1 - y, low, :], plane, 1)
 
@@ -182,14 +183,14 @@
         pl.when(z + step < line)(lambda: visit(z + step, DOWN))
 
     def along_line(step, wait, act):
-        for part in range(2):
+        for part in range(pieces):
 
             def one_piece(plane, kind):
                 ref = piece(c, plane, y, part)
                 wait(LINE, ref, plane, part)
                 act(kind, ref, plane, part)
                 act(ACROSS, ref, plane, part)
-                if part == 1:
+                if part == pieces - 1:
                     act(SIBLING, blocks.at[c, plane, y, low, :], plane, 0)
 
             sides(step, one_piece)
@@ -197,9 +198,9 @@
     def rest_of_line(step, wait, act):
         def the_rest(plane, kind):
             ref = both_rest(c, plane)
-            wait(LINE, ref, plane, 2)
-            act(kind, ref, plane, 2)
-            act(SIBLING, ref, plane, 2)
+            wait(LINE, ref, plane, pieces)
+            act(kind, ref, plane, pieces)
+            act(SIBLING, ref, plane, pieces)
 
         sides(step, the_rest)
 
@@ -216,7 +217,7 @@
             def _():
                 arrive(SIBLING, blocks.at[1 - c, plane, y, low, :], plane, 0)
                 arrive(SIBLING, blocks.at[1 - c, plane, 1 - y, low, :], plane, 1)
-                arrive(SIBLING, both_rest(1 - c, plane), plane, 2)
+                arrive(SIBLING, both_rest(1 - c, plane), plane, pieces)
 
             half(plane, (c + h) % 2)
             return carry
@@ -330,7 +331,7 @@
 
 def body(narrow, wide, state, in_pattern, out_pattern):
     rows, cols = state.shape
-    cut = 2 * rows // 5
+    cut = (0, 3 * rows // 10, 6 * rows // 10, 8 * rows // 10)
     line = wide // 4
     hbm = pl.BlockSpec(memory_space=pltpu.HBM)
     vmem = pl.BlockSpec(memory_space=pltpu.VMEM)
@@ -349,8 +350,8 @@
             pltpu.VMEM((rows, cols), jnp.float32),
             pltpu.VMEM((narrow, 8, LANES), jnp.float32),
             pltpu.SemaphoreType.DMA((3,)),
-            pltpu.SemaphoreType.DMA((4, line, 3)),
-            pltpu.SemaphoreType.DMA((3, line, 3)),
+            pltpu.SemaphoreType.DMA((4, line, 4)),
+            pltpu.SemaphoreType.DMA((3, line, 4)),
             pltpu.SemaphoreType.DMA((narrow,)),
             pltpu.SemaphoreType.DMA((narrow,)),
             pltpu.SemaphoreType.DMA((narrow,)),

time: 29.2 us -> 28.9 us (0.990)
  Pallas kernels: 28.4 us -> 28.1 us
    pallas_call x1, Pallas kernels: 28.4 us -> 28.1 us  [body(): pl.pallas_call(functools.partial(kernel, narrow, wide, cut), out_shape=pl...]
where the time goes in v10:
time: 28.9 us; the launch traced here: 28.7 us
  Pallas kernels  28.1 us (97%)
  local copies, waits for them, and re-layouts  0.68 us (2%)
    pallas_call x1, Pallas kernels, body(): pl.pallas_call(functools.partial(kernel, narrow, wide, cut), out_shape=pl...  28.1 us
    unnamed x1, local copies, waits for them, and re-layouts  0.68 us

profile of v10, /device:TPU:0, one launch (start us, length us, event | category | flops | bytes accessed | tf_op | source)
XLA Modules:
  0.0 28.7 jit_solution(16858453642352327587)
XLA Ops:
  0.0 28.1 %shard_map.37 = f32[80,640]{1,0:T(8,128)S(1)} custom-call(s32[5,5]{1,0:T(8,128)} %in_hbm.1, s32[5,5]{1,0:T(8,128)} %out_hbm.1, f32[80,640]{1,0:T(8,128)} %x_hbm.1), custom_call_target="tpu_custom_call" | custom-call | flops 131072000 | bytes 409600 | tf_op jit(solution)/shard_map/pallas_call | solution.py:339
  28.1 0.7 %copy.5 = f32[80,640]{1,0:T(8,128)} copy(f32[80,640]{1,0:T(8,128)S(1)} %shard_map.37) | data formatting | bytes 409600

commit v11 on v10

--- a/solution.py
+++ b/solution.py
@@ -331,7 +331,7 @@
 
 def body(narrow, wide, state, in_pattern, out_pattern):
     rows, cols = state.shape
-    cut = (0, 3 * rows // 10, 6 * rows // 10, 8 * rows // 10)
+    cut = (0, 4 * rows // 10, 7 * rows // 10, 9 * rows // 10)
     line = wide // 4
     hbm = pl.BlockSpec(memory_space=pltpu.HBM)
     vmem = pl.BlockSpec(memory_space=pltpu.VMEM)

time: 28.9 us -> 29.1 us (level)
  no operation moved by 1% of the time
where the time goes in v11:
time: 29.1 us; the launch traced here: 29 us
  Pallas kernels  28.3 us (97%)
  local copies, waits for them, and re-layouts  0.68 us (2%)
    pallas_call x1, Pallas kernels, body(): pl.pallas_call(functools.partial(kernel, narrow, wide, cut), out_shape=pl...  28.3 us
    unnamed x1, local copies, waits for them, and re-layouts  0.68 us

profile of v11, /device:TPU:0, one launch (start us, length us, event | category | flops | bytes accessed | tf_op | source)
XLA Modules:
  0.0 29.0 jit_solution(10795056446654218976)
XLA Ops:
  0.0 28.3 %shard_map.37 = f32[80,640]{1,0:T(8,128)S(1)} custom-call(s32[5,5]{1,0:T(8,128)} %in_hbm.1, s32[5,5]{1,0:T(8,128)} %out_hbm.1, f32[80,640]{1,0:T(8,128)} %x_hbm.1), custom_call_target="tpu_custom_call" | custom-call | flops 131072000 | bytes 409600 | tf_op jit(solution)/shard_map/pallas_call | solution.py:339
  28.3 0.7 %copy.5 = f32[80,640]{1,0:T(8,128)} copy(f32[80,640]{1,0:T(8,128)S(1)} %shard_map.37) | data formatting | bytes 409600
